TPU v7x, 32 devices: a whole 2x2x4 slice. The times are simulated.
32 devices in a mesh: groups: 2 (over y), lists: 8 (over z, x), sub: 2 (over core).
Axes of the slice: x: 2, y: 2, z: 4, core: 2. Of those that a mesh axis runs over, the one named last changes fastest.
Arguments:
- tokens: bfloat16 [3072, 8, 1024], P(('groups', 'lists', 'sub')), parts along dimension 0, may hold values from -6 to 6
- w_in: bfloat16 [1024, 2048], replicated, may hold values from -0.1875 to 0.1875
- w_out: bfloat16 [2048, 1024], replicated, may hold values from -0.125 to 0.125
- gain: float32 [1024], replicated, may hold values from 0.1 to 1.9
- centroids: bfloat16 [65536, 1024], P(('lists', 'sub')), may hold values from -6 to 6
- list_slot: int32 [131072], P('groups'), parts along dimension 0, may hold values from 0 to 65535, as said below
- assign: int32 [3072], P(('groups', 'lists', 'sub')), parts along dimension 0, may hold values from 0 to 65535, as said below
- codes: int32 [3072, 64], P(('groups', 'lists', 'sub')), parts along dimension 0, may hold values from 0 to 255, as said below
- list_weight: float32 [131072], P('groups'), parts along dimension 0, may hold values from 0.25 to 4
Outputs:
- updated_centroids: bfloat16 [131072, 1024], P(('groups', 'lists', 'sub')), parts along dimension 0
- codewords: float32 [512, 1024], P(('groups', 'lists', 'sub')), parts along dimension 0
There are 2 independent parts, one for each index of `groups`. A program takes and returns all parts, laid end to end along the dimension named above; an argument that names none is the same for every part. Nothing has to cross between parts.
Inputs may be any that keep to these rules, and one draw needn't show every extreme that they name: In every aligned block of 96 passages, at most 12 have slots list_slot[assign] within one device's block of 4096 slots, and in every block some device's slots take exactly 12. In every aligned block of 96 passages, at most 768 of its codes name codewords within one device's block of codewords, and in every block some device's codewords take exactly 768. `list_slot`: each slot once.
All inputs are finite; a program needn't handle non-finite values.
Results may differ from a plain program's by a relative error of at most 0.0023.
Values may be sent and summed in bfloat16 or wider, within the bound.
A program may use at most 128 MiB of HBM per device.

v0:
```python
import math

import jax
import jax.numpy as jnp
from jax import lax
from jax.sharding import PartitionSpec as P

CODES = 256


def encode(block, w_in, w_out, gain):
    count, length, width = block.shape
    flat = block.reshape(count * length, width)
    hidden = jax.nn.gelu(
        jnp.dot(flat, w_in, preferred_element_type=jnp.float32), approximate=True
    ).astype(jnp.bfloat16)
    mixed = flat.astype(jnp.float32) + jnp.dot(hidden, w_out, preferred_element_type=jnp.float32)
    centre = mixed - jnp.mean(mixed, axis=-1, keepdims=True)
    spread = jnp.mean(centre * centre, axis=-1, keepdims=True)
    normed = centre * lax.rsqrt(spread + 1e-05) * gain
    averaged = jnp.mean(normed.reshape(count, length, width), axis=1)
    scale = lax.rsqrt(jnp.mean(averaged * averaged, axis=-1, keepdims=True) + 1e-06)
    return (averaged * scale).astype(jnp.bfloat16)


def pack_codes(codes):
    rows, parts = codes.shape
    quads = codes.reshape(rows, parts // 4, 4)
    low = quads[:, :, 0] + 256 * quads[:, :, 1] + 65536 * quads[:, :, 2]
    return low + (quads[:, :, 3] - 128) * 16777216


def unpack_codes(packed):
    rows, words = packed.shape
    top = packed // 16777216
    low = packed - top * 16777216
    third = low // 65536
    rest = low - third * 65536
    second = rest // 256
    first = rest - second * 256
    stacked = jnp.stack([first, second, third, top + 128], axis=-1)
    return stacked.reshape(rows, words * 4).astype(jnp.int32)


def code_table(codes, plus, minus, weight, n_codes):
    rows, width = plus.shape
    parts = codes.shape[1]
    sub_width = width // parts
    block = math.gcd(rows, 256)
    turns = rows // block

    def step(index, carry):
        sums, counts = carry
        start = index * block
        code_blk = lax.dynamic_slice_in_dim(codes, start, block, 0)
        value_blk = lax.dynamic_slice_in_dim(plus, start, block, 0).astype(jnp.float32)
        value_blk = value_blk - lax.dynamic_slice_in_dim(minus, start, block, 0).astype(jnp.float32)
        value_blk = value_blk.reshape(block, parts, sub_width)
        weight_blk = lax.dynamic_slice_in_dim(weight, start, block, 0)
        onehot = (
            code_blk[:, :, None] == jnp.arange(n_codes, dtype=jnp.int32)[None, None, :]
        ).astype(jnp.float32) * weight_blk[:, None, None]
        sums = sums + jnp.einsum("rmc,rmk->cmk", onehot, value_blk, precision=lax.Precision.HIGHEST)
        counts = counts + jnp.sum(onehot, axis=0).T
        return (sums, counts)

    start_val = (
        jnp.zeros((n_codes, parts, sub_width), jnp.float32),
        jnp.zeros((n_codes, parts), jnp.float32),
    )
    sums, counts = lax.fori_loop(0, turns, step, start_val)
    return (sums.reshape(n_codes, width), counts)


def earlier_equal(target):
    count = target.shape[-1]
    same = target[..., :, None] == target[..., None, :]
    before = (
        jnp.arange(count, dtype=jnp.int32)[None, :] < jnp.arange(count, dtype=jnp.int32)[:, None]
    )
    return jnp.sum((same & before).astype(jnp.int32), axis=-1)


def shards(tokens, w_in, w_out, gain, centroids, list_slot, assign, codes, list_weight):
    pooled = encode(tokens, w_in, w_out, gain)
    own_rows, width = pooled.shape
    parts = codes.shape[1]
    slots_dev = centroids.shape[0]
    devices = lax.axis_size(("lists", "sub"))
    index = lax.axis_index(("lists", "sub"))
    base = index * slots_dev
    row_cap = max(2, (2 * own_rows + devices - 1) // devices)
    target = jnp.take(list_slot, assign) // slots_dev
    rank = earlier_equal(target)
    packed = pack_codes(codes)
    dest = target * row_cap + rank
    row_buf = jnp.zeros((devices * row_cap, width), jnp.bfloat16).at[dest].set(pooled)
    id_buf = jnp.full((devices * row_cap,), -1, jnp.int32).at[dest].set(assign)
    code_buf = jnp.zeros((devices * row_cap, parts // 4), jnp.int32).at[dest].set(packed)
    got_rows, got_ids, got_codes = (
        lax.all_to_all(
            row_buf.reshape(devices, row_cap, width),
            ("lists", "sub"),
            split_axis=0,
            concat_axis=0,
            tiled=True,
        ),
        lax.all_to_all(
            id_buf.reshape(devices, row_cap),
            ("lists", "sub"),
            split_axis=0,
            concat_axis=0,
            tiled=True,
        ),
        lax.all_to_all(
            code_buf.reshape(devices, row_cap, parts // 4),
            ("lists", "sub"),
            split_axis=0,
            concat_axis=0,
            tiled=True,
        ),
    )
    rows = got_rows.reshape(devices * row_cap, width)
    list_ids = got_ids.reshape(devices * row_cap)
    row_codes = unpack_codes(got_codes.reshape(devices * row_cap, parts // 4))
    safe_ids = jnp.maximum(list_ids, 0)
    local = jnp.take(list_slot, safe_ids) - base
    mine = (list_ids >= 0) & (local >= 0) & (local < slots_dev)
    onehot = (
        (local[:, None] == jnp.arange(slots_dev, dtype=jnp.int32)[None, :]) & mine[:, None]
    ).astype(jnp.bfloat16)
    list_sums = lax.dot_general(
        onehot, rows, (((0,), (0,)), ((), ())), preferred_element_type=jnp.float32
    )
    list_counts = jnp.sum(onehot.astype(jnp.float32), axis=0)
    updated = (
        centroids + (list_sums - list_counts[:, None] * centroids) / (list_counts[:, None] + 1.0)
    ).astype(jnp.bfloat16)
    cent_rows = jnp.dot(onehot, centroids)
    weight = jnp.take(list_weight, safe_ids) * mine.astype(jnp.float32)
    n_codes = CODES
    sums, counts = code_table(row_codes, rows, cent_rows, weight, n_codes)
    part_sums, part_counts = (
        lax.psum_scatter(sums, ("lists", "sub"), scatter_dimension=0, tiled=True),
        lax.psum_scatter(counts, ("lists", "sub"), scatter_dimension=0, tiled=True),
    )
    held = part_sums.shape[0]
    shaped = (
        part_sums.reshape(held, parts, width // parts) / jnp.maximum(part_counts, 1.0)[:, :, None]
    )
    return (updated, shaped.reshape(held, width))


def solution(mesh):
    return jax.shard_map(
        shards,
        mesh=mesh,
        in_specs=(
            P(("groups", "lists", "sub"), None, None),
            P(),
            P(),
            P(),
            P(("lists", "sub"), None),
            P("groups"),
            P(("groups", "lists", "sub")),
            P(("groups", "lists", "sub"), None),
            P("groups"),
        ),
        out_specs=(P(("groups", "lists", "sub"), None), P(("groups", "lists", "sub"), None)),
        check_vma=False,
    )
```

profile of v0, /device:TPU:0, one launch (start us, length us, event | category | flops | bytes accessed | tf_op | source)
XLA Modules:
  0.0 206.9 jit_solution(16734145190178804178)
XLA Ops:
  7.2 0.7 compare_select_fusion.1
  7.9 0.2 copy-done
  8.1 1.1 gather_fusion
  9.3 0.7 and_select_fusion
  10.0 0.2 convert_reduce_fusion.1
  10.1 1.0 scatter_custom_fusion
  11.2 0.7 all_to_all.12
  11.8 7.4 %all-to-all-start = ((s32[16,1,12]{2,1,0:T(1,128)}), s32[16,1,12]{2,1,0:T(1,128)S(1)}, u32[]{:S(2)}, u32[]{:S(2)}) async-start(s32[16,1,12]{2,1,0:T(1,128)} %bitcast), calls=%async_computation | async-start | bytes 16384 | tf_op jit(solution)/shard_map/all_to_all | solution.py:108
  19.2 0.9 fusion.73
  20.2 11.2 %fusion.74 = (f32[768]{0:T(1024)S(1)}, f32[768,1024]{1,0:T(8,128)S(1)}) fusion(bf16[2048,1024]{1,0:T(8,128)(2,1)} %param.13, bf16[1024,2048]{1,0:T(8,128)(2,1)} %param.12, bf16[96,8,1024]{2,1,0:T(8,128)(2,1)} %param.11), kind=kOutput, calls=%fused_computation.124 | convolution fusion | flops 6458964992 | bytes 13110272 | tf_op jit(solution)/shard_map/dot_general | solution.py:17
  31.4 0.4 multiply_reduce_fusion
  31.8 1.1 bitcast_reduce_fusion
  33.0 0.7 copy-done.1
  33.7 0.1 multiply_reduce_fusion.1
  33.8 0.1 copy.93
  33.9 0.1 copy.94
  34.0 0.1 copy.92
  34.1 0.1 copy.95
  34.2 0.9 scatter_custom_fusion.2
  35.1 0.2 copy.77
  35.3 0.7 reshape.503
  36.0 1.7 scatter_custom_fusion.1
  37.7 0.9 reshape.421
  38.6 6.0 %all-to-all-start.2 = ((s32[16,1,192]{2,1,0:T(1,128)}), s32[16,1,192]{2,1,0:T(1,128)S(1)}, u32[]{:S(2)}, u32[]{:S(2)}) async-start(s32[16,1,192]{2,1,0:T(1,128)} %reshape.503), calls=%async_computation.2 | async-start | bytes 32768 | tf_op jit(solution)/shard_map/all_to_all | solution.py:115
  44.6 0.1 reshape.438
  44.7 0.1 ge.39
  44.8 0.1 le.38
  45.0 1.4 gather_fusion.1
  46.4 2.2 %gather_fusion.2 = f32[192]{0:T(256)S(1)} fusion(f32[65536]{0:T(1024)} %param.19, s32[1024]{0:T(1024)S(1)} %pad_clamp_fusion), kind=kCustom, calls=%fused_computation.2 | custom fusion | bytes 2304 | tf_op jit(solution)/shard_map/jit(_take)/gather | solution.py:140
  48.6 2.4 %all-to-all-done.2 = s32[16,1,192]{2,1,0:T(1,128)S(1)} async-done(((s32[16,1,192]{2,1,0:T(1,128)}), s32[16,1,192]{2,1,0:T(1,128)S(1)}, u32[]{:S(2)}, u32[]{:S(2)}) %all-to-all-start.2) | async-done | bytes 12320 | tf_op jit(solution)/shard_map/all_to_all | solution.py:115
  51.1 3.6 %all-to-all-start.1 = ((bf16[16,12,1024]{2,1,0:T(8,128)(2,1)}), bf16[16,12,1024]{2,1,0:T(8,128)(2,1)S(1)}, u32[]{:S(2)}, u32[]{:S(2)}) async-start(bf16[16,12,1024]{2,1,0:T(8,128)(2,1)} %reshape.421), calls=%async_computation.1 | async-start | bytes 1048576 | tf_op jit(solution)/shard_map/all_to_all | solution.py:101
  54.6 0.2 reduce-scatter.9.cloned.1.call-start
  54.9 7.0 %fusion.26 = bf16[192,1024]{0,1:T(8,128)(2,1)S(1)} fusion(bf16[4096,1024]{1,0:T(8,128)(2,1)} %param.15, s32[192]{0:T(256)S(1)} %get-tuple-element.224, pred[192]{0:T(512)(128)(4,1)S(1)} %get-tuple-element.223), kind=kOutput, calls=%fused_computation.41 | convolution fusion | flops 1612185600 | bytes 8782784 | tf_op jit(solution)/shard_map/dot_general | solution.py:139
  61.9 0.7 convert_reduce_fusion
  62.6 0.5 broadcast.602
  63.1 0.7 reduce.8
  63.8 0.1 reshape.504
  64.0 0.1 reshape.425
  64.2 4.9 %all-to-all-done.1 = bf16[16,12,1024]{2,1,0:T(8,128)(2,1)S(1)} async-done(((bf16[16,12,1024]{2,1,0:T(8,128)(2,1)}), bf16[16,12,1024]{2,1,0:T(8,128)(2,1)S(1)}, u32[]{:S(2)}, u32[]{:S(2)}) %all-to-all-start.1) | async-done | bytes 393248 | tf_op jit(solution)/shard_map/all_to_all | solution.py:101
  69.1 0.1 reshape.422
  69.2 13.8 %while.16 = (s32[]{:T(128)}, f32[256,64,16]{0,2,1:T(8,128)S(1)}, f32[256,64]{0,1:T(8,128)S(1)}, bf16[192,1024]{1,0:T(8,128)(2,1)S(1)}, bf16[192,1024]{0,1:T(8,12...) while((s32[]{:T(128)}, f32[256,64,16]{0,2,1:T(8,128)S(1)}, ...), condition=%wide.region_11.12_spmd.clone, body=%wide.region_9.11_spmd.clone.sunk | while | flops 207306752 | bytes 3736766 | solution.py:71
  69.2 0.1 dynamic_slice.42
  69.4 1.2 select_reduce_fusion.2
  70.7 0.2 copy.97
  70.9 0.1 convert_subtract_fusion.2
  71.0 2.8 %fusion.87 = f32[256,64,16]{0,2,1:T(8,128)S(1)} fusion(f32[64,64,16]{0,2,1:T(8,128)S(1)} %bitcast.49, f32[64]{0:T(128)S(1)} %dynamic_slice.42, s32[64,64]{0,1:T(8,128)S(1)} %constant_dynamic-slice_fusion.5, f32[256,64,16]{0,2,1:T(8,128)S(1)} %get-tuple-element.290, pred[]{:T(512)S(6)} %compare.73), kind=kOutput, calls=%fused_computation.14.clone.1 | convolution fusion | flops 203948032 | bytes 2375937 | tf_op jit(solution)/shard_map/while/body/eval_jaxpr/rmc,rmk->cmk/dot_general | solution.py:63
  73.8 0.1 dynamic_slice.42
  74.0 1.2 select_reduce_fusion.2
  75.3 0.2 copy.97
  75.5 0.1 convert_subtract_fusion.2
  75.6 2.8 %fusion.87 = f32[256,64,16]{0,2,1:T(8,128)S(1)} fusion(f32[64,64,16]{0,2,1:T(8,128)S(1)} %bitcast.49, f32[64]{0:T(128)S(1)} %dynamic_slice.42, s32[64,64]{0,1:T(8,128)S(1)} %constant_dynamic-slice_fusion.5, f32[256,64,16]{0,2,1:T(8,128)S(1)} %get-tuple-element.290, pred[]{:T(512)S(6)} %compare.73), kind=kOutput, calls=%fused_computation.14.clone.1 | convolution fusion | flops 203948032 | bytes 2375937 | tf_op jit(solution)/shard_map/while/body/eval_jaxpr/rmc,rmk->cmk/dot_general | solution.py:63
  78.6 1.2 select_reduce_fusion.2
  79.9 0.2 copy.97
  80.1 0.1 convert_subtract_fusion.2
  80.2 2.8 %fusion.87 = f32[256,64,16]{0,2,1:T(8,128)S(1)} fusion(f32[64,64,16]{0,2,1:T(8,128)S(1)} %bitcast.49, f32[64]{0:T(128)S(1)} %dynamic_slice.42, s32[64,64]{0,1:T(8,128)S(1)} %constant_dynamic-slice_fusion.5, f32[256,64,16]{0,2,1:T(8,128)S(1)} %get-tuple-element.290, pred[]{:T(512)S(6)} %compare.73), kind=kOutput, calls=%fused_computation.14.clone.1 | convolution fusion | flops 203948032 | bytes 2375937 | tf_op jit(solution)/shard_map/while/body/eval_jaxpr/rmc,rmk->cmk/dot_general | solution.py:63
  83.0 0.7 copy.89
  83.9 1.3 copy.87
  85.2 8.9 %fusion.14 = bf16[4096,1024]{1,0:T(8,128)(2,1)} fusion(bf16[4096,1024]{1,0:T(8,128)(2,1)} %param.15, bf16[192,1024]{1,0:T(8,128)(2,1)S(1)} %get-tuple-element.315, f32[4096]{0:T(1024)S(1)} %broadcast_add_fusion, f32[4096]{0:T(1024)S(1)} %convert_reduce_fusion, s32[192]{0:T(256)S(1)} %get-tuple-element.224, pred[192]{0:T(512)(128)(4,1)S(1)} %get-tuple-element.223), kind=kOutput, calls=%fused_computation.24 | convolution fusion | flops 1637351424 | bytes 17204160 | tf_op jit(solution)/shard_map/dot_general | solution.py:132
  94.1 44.3 %reduce-scatter.9.cloned.1.call-done = f32[16,64]{1,0:T(8,128)} async-done(((f32[256,64]{1,0:T(8,128)}), f32[16,64]{1,0:T(8,128)}) %reduce-scatter.9.cloned.1.call-update) | async-done | bytes 4112 | tf_op jit(solution)/shard_map/reduce_scatter | solution.py:145
  138.5 0.7 broadcast_maximum_fusion
  139.2 0.2 div.105
  139.4 0.3 div.106
  139.7 58.9 %reduce-scatter.7.cloned.1.call-done = f32[16,1024]{1,0:T(8,128)} async-done(((f32[256,1024]{1,0:T(8,128)}), f32[16,1024]{1,0:T(8,128)}) %reduce-scatter.7.cloned.1.call-update) | async-done | bytes 65552 | tf_op jit(solution)/shard_map/reduce_scatter | solution.py:144
  198.5 1.5 div.107
  (38 shorter events, 0.8 us)
Async XLA Ops:
  7.2 1.0 copy-start
  11.8 26.7 %all-to-all-start = ((s32[16,1,12]{2,1,0:T(1,128)}), s32[16,1,12]{2,1,0:T(1,128)S(1)}, u32[]{:S(2)}, u32[]{:S(2)}) async-start(s32[16,1,12]{2,1,0:T(1,128)} %bitcast), calls=%async_computation | async-start | bytes 16384 | tf_op jit(solution)/shard_map/all_to_all | solution.py:108
  20.2 11.6 %copy-start.3 = (f32[1024]{0:T(1024)S(1)}, f32[1024]{0:T(1024)}, u32[]{:S(2)}) copy-start(f32[1024]{0:T(1024)} %param.14) | copy-start | bytes 12292
  33.0 0.7 copy-start.1
  38.6 12.5 %all-to-all-start.2 = ((s32[16,1,192]{2,1,0:T(1,128)}), s32[16,1,192]{2,1,0:T(1,128)S(1)}, u32[]{:S(2)}, u32[]{:S(2)}) async-start(s32[16,1,192]{2,1,0:T(1,128)} %reshape.503), calls=%async_computation.2 | async-start | bytes 32768 | tf_op jit(solution)/shard_map/all_to_all | solution.py:115
  51.1 18.1 %all-to-all-start.1 = ((bf16[16,12,1024]{2,1,0:T(8,128)(2,1)}), bf16[16,12,1024]{2,1,0:T(8,128)(2,1)S(1)}, u32[]{:S(2)}, u32[]{:S(2)}) async-start(bf16[16,12,1024]{2,1,0:T(8,128)(2,1)} %reshape.421), calls=%async_computation.1 | async-start | bytes 1048576 | tf_op jit(solution)/shard_map/all_to_all | solution.py:101
  54.6 83.8 %reduce-scatter.9.cloned.1.call-start = ((), (), s32[]{:S(2)}) async-start(), calls=%async_computation.6 | async-start | bytes 139264 | tf_op jit(solution)/shard_map/reduce_scatter | solution.py:145
  54.9 14.3 %copy-start.2 = (f32[256,64,16]{0,2,1:T(8,128)S(1)}, f32[256,64,16]{0,2,1:T(8,128)}, u32[]{:S(2)}) copy-start(f32[256,64,16]{0,2,1:T(8,128)} %custom-call) | copy-start | bytes 3145732
  83.8 114.7 %reduce-scatter.7.cloned.1.call-start = ((), (), s32[]{:S(2)}) async-start(), calls=%async_computation.5 | async-start | bytes 1114112 | tf_op jit(solution)/shard_map/reduce_scatter | solution.py:144
Sparse Core Ops, SparseCore 0:
  83.9 54.5 reduce-scatter.8
  142.1 56.3 reduce-scatter.6
where the time goes:
time: 207 us
  waiting for transfers between devices  111 us (54%)
  matrix products  35.4 us (17%)
  starting transfers between devices  17.2 us (8%)
  local copies, waits for them, and re-layouts  15.4 us (7%)
  between operations  14.4 us (7%)
  other arithmetic  13.8 us (7%)
    reduce_scatter x1, waiting for transfers between devices, shards(): lax.psum_scatter(sums, ('lists', 'sub'), scatter_dimension=0, tiled=True)  58.9 us
    reduce_scatter x1, waiting for transfers between devices, shards(): lax.psum_scatter(counts, ('lists', 'sub'), scatter_dimension=0, tiled=True)  44.3 us
    dot_general x1, matrix products, encode(): jnp.dot(hidden, w_out, preferred_element_type=jnp.float32)  11.2 us
    dot_general x1, matrix products, shards(): lax.dot_general(onehot, rows, (((0,), (0,)), ((), ())), preferred_element...  8.92 us
    dot_general x3, matrix products, step(): jnp.einsum('rmc,rmk->cmk', onehot, value_blk, precision=lax.Precision.HIG...  8.32 us
    all_to_all x1, starting transfers between devices, shards(): lax.all_to_all(id_buf.reshape(devices, row_cap), ('lists', 'sub'), split_...  7.36 us
    dot_general x1, matrix products, shards(): cent_rows = jnp.dot(onehot, centroids)  6.97 us
    all_to_all x1, starting transfers between devices, shards(): lax.all_to_all(code_buf.reshape(devices, row_cap, parts // 4), ('lists',...  6 us
  transfers between devices with their start and end apart: 5, of which 4 were waited for; matrix products, arithmetic and copies ran while one was open for 21% of the time, Pallas kernels for 0%

commit v1 on v0

v1 whole, which is shorter than its diff:
```python
import functools

import jax
import jax.numpy as jnp
from jax import lax
from jax.experimental import pallas as pl
from jax.experimental.pallas import tpu as pltpu
from jax.sharding import PartitionSpec as P

CODES = 256
LANES = 128
SUB = 16
BF, F32, I32 = jnp.bfloat16, jnp.float32, jnp.int32
MESH = pl.DeviceIdType.MESH


def up(value, step):
    return (value + step - 1) // step * step


def gelu(x):
    inner = x * (0.7978845608028654 + 0.035677408136300125 * (x * x))
    return 0.5 * x * (1.0 + jnp.tanh(inner))


def main_kernel(
    cfg,
    slot_row_ref, slot_col_ref, weight_ref, codes_ref, gain_ref,
    tok_hbm, win_hbm, wout_hbm, cent_hbm,
    rows_out, ids_out, code_out,
    tok, win, wout, cent, pooled,
    ids_send, ids_got, cent_send, cent_got, row_send, row_got,
    table, table16, got1, send2, got2, send3, got3,
    load_sem, id_s, id_r, cent_s, cent_r, row_s, row_r, t_s, t_r,
):
    L, S, lo, hi, cap, capp, slots_dev, held, heldp = cfg
    D = L * S
    width = tok.shape[1]
    passages = tok.shape[0] // 8
    padded = slot_row_ref.shape[1]
    li, si = lax.axis_index("lists"), lax.axis_index("sub")
    me = li * S + si
    hi_i, lo_i = li // lo, lax.rem(li, lo)
    ff = win.shape[1]
    nchunk = 4
    fc = ff // nchunk

    def dev(index):
        return {"lists": index // S, "sub": lax.rem(index, S)}

    loads = [pltpu.make_async_copy(tok_hbm, tok, load_sem.at[0])]
    for c in range(nchunk):
        loads.append(pltpu.make_async_copy(
            win_hbm.at[:, pl.ds(c * fc, fc)], win.at[:, pl.ds(c * fc, fc)], load_sem.at[1 + 2 * c]))
        loads.append(pltpu.make_async_copy(
            wout_hbm.at[pl.ds(c * fc, fc), :], wout.at[pl.ds(c * fc, fc), :], load_sem.at[2 + 2 * c]))
    cent_load = pltpu.make_async_copy(cent_hbm, cent, load_sem.at[1 + 2 * nchunk])
    for one in loads:
        one.start()
    cent_load.start()

    barrier = pltpu.get_barrier_semaphore()

    def greet(j, carry):
        pl.semaphore_signal(barrier, inc=1, device_id=dev(lax.rem(me + j, D)), device_id_type=MESH)
        return carry

    lax.fori_loop(1, D, greet, 0)

    shift = slots_dev.bit_length() - 1
    slot_row, slot_col = slot_row_ref[...], slot_col_ref[...]
    tr = jnp.where(slot_row >= 0, lax.shift_right_logical(slot_row, shift), -1)
    tc = jnp.where(slot_col >= 0, lax.shift_right_logical(slot_col, shift), -1)
    i0 = lax.broadcasted_iota(I32, (padded, padded), 0)
    i1 = lax.broadcasted_iota(I32, (padded, padded), 1)
    same = tr == tc
    rank_row = jnp.sum(jnp.where(same & (i0 < i1), 1.0, 0.0), axis=0, keepdims=True).astype(I32)
    rank_col = jnp.sum(jnp.where(same & (i1 < i0), 1.0, 0.0), axis=1, keepdims=True).astype(I32)
    dest_row = jnp.where(tr >= 0, tr * capp + rank_row, -1)
    dest_col = jnp.where(tc >= 0, tc * capp + rank_col, -1)
    local_row = (slot_row - jnp.maximum(tr, 0) * slots_dev + 1).astype(F32)
    di = lax.broadcasted_iota(I32, (D * capp, padded), 0)
    spread = di == dest_row
    ids = jnp.sum(jnp.where(spread, local_row, 0.0), axis=1, keepdims=True).astype(I32) - 1
    ids_send[...] = jnp.broadcast_to(ids, (D * capp, LANES)).reshape(D, capp, LANES)
    ids_got[me] = ids_send[me]

    pl.semaphore_wait(barrier, D - 1)

    def exchange(send, got, ss, rs):
        def start(j, carry):
            to = lax.rem(me + j, D)
            pltpu.make_async_remote_copy(
                src_ref=send.at[to], dst_ref=got.at[me], send_sem=ss.at[j], recv_sem=rs.at[j],
                device_id=dev(to), device_id_type=MESH).start()
            return carry

        lax.fori_loop(1, D, start, 0)

        def finish_recv():
            def body(j, carry):
                frm = lax.rem(me + D - j, D)
                pltpu.make_async_remote_copy(
                    src_ref=send.at[frm], dst_ref=got.at[frm], send_sem=ss.at[j],
                    recv_sem=rs.at[j], device_id=dev(frm), device_id_type=MESH).wait_recv()
                return carry
            lax.fori_loop(1, D, body, 0)

        def finish_send():
            def body(j, carry):
                to = lax.rem(me + j, D)
                pltpu.make_async_remote_copy(
                    src_ref=send.at[to], dst_ref=got.at[me], send_sem=ss.at[j],
                    recv_sem=rs.at[j], device_id=dev(to), device_id_type=MESH).wait_send()
                return carry
            lax.fori_loop(1, D, body, 0)

        return finish_recv, finish_send

    id_recv, id_sent = exchange(ids_send, ids_got, id_s, id_r)

    nblk = 3 if passages % 48 == 0 else 1
    per = passages // nblk
    toks = per * 8

    def encode(b, wait):
        x = tok[pl.ds(b * toks, toks), :]
        acc = x.astype(F32)
        for c in range(nchunk):
            if wait:
                loads[1 + 2 * c].wait()
            h = gelu(jnp.dot(x, win[:, c * fc:(c + 1) * fc], preferred_element_type=F32)).astype(BF)
            if wait:
                loads[2 + 2 * c].wait()
            acc = acc + jnp.dot(h, wout[c * fc:(c + 1) * fc, :], preferred_element_type=F32)
        centre = acc - jnp.mean(acc, axis=-1, keepdims=True)
        var = jnp.mean(centre * centre, axis=-1, keepdims=True)
        normed = centre * lax.rsqrt(var + 1e-05)
        avg = jnp.mean(normed.reshape(per, 8, width), axis=1) * gain_ref[...]
        scale = lax.rsqrt(jnp.mean(avg * avg, axis=-1, keepdims=True) + 1e-06)
        pooled[pl.ds(b * per, per), :] = (avg * scale).astype(BF)

    pooled[...] = jnp.zeros_like(pooled)
    loads[0].wait()
    encode(0, True)

    id_recv()
    cent_load.wait()
    want = ids_got[...].reshape(D * capp, LANES)
    ids_out[...] = want.T[0:8, :]
    rb = 256

    def pick(i, carry):
        start = pl.multiple_of(i * rb, rb)
        mine = ids_got[pl.ds(i * (rb // capp), rb // capp)].reshape(rb, LANES)[:, 0:1]
        hit = jnp.where(lax.broadcasted_iota(I32, (rb, slots_dev), 1) == mine, 1.0, 0.0).astype(BF)
        out = jnp.dot(hit, cent[...], preferred_element_type=F32).astype(BF)
        cent_send[pl.ds(i * (rb // capp), rb // capp)] = out.reshape(rb // capp, capp, width)
        return carry

    lax.fori_loop(0, D * capp // rb, pick, 0)
    cent_got[me] = cent_send[me]
    cent_recv, cent_sent = exchange(cent_send, cent_got, cent_s, cent_r)

    for b in range(1, nblk):
        encode(b, False)

    put = jnp.where(spread, 1.0, 0.0).astype(BF)
    row_send[...] = jnp.dot(put, pooled[...], preferred_element_type=F32).astype(BF).reshape(D, capp, width)
    row_got[me] = row_send[me]

    cent_recv()
    get = jnp.where(
        lax.broadcasted_iota(I32, (padded, D * capp), 1) == dest_col, 1.0, 0.0).astype(BF)
    cent_rows = jnp.dot(get, cent_got[...].reshape(D * capp, width), preferred_element_type=F32)
    weight = weight_ref[...]
    resid = ((pooled[...].astype(F32) - cent_rows) * weight).astype(BF)
    w_hi = weight.astype(BF).astype(F32)
    w_lo = weight - w_hi

    nrow = S * lo * hi * heldp
    tb = 256
    lane = lax.broadcasted_iota(I32, (padded, LANES), 1)
    group = LANES // SUB
    ngroup = width // LANES
    logical = {"hp": heldp.bit_length() - 1}

    def build(i, carry):
        t = lax.broadcasted_iota(I32, (tb, 1), 0) + i * tb
        k = jnp.bitwise_and(t, heldp - 1)
        rest = lax.shift_right_logical(t, logical["hp"])
        h = jnp.bitwise_and(rest, hi - 1)
        rest = lax.shift_right_logical(rest, hi.bit_length() - 1)
        l = jnp.bitwise_and(rest, lo - 1)
        s = lax.shift_right_logical(rest, lo.bit_length() - 1)
        code = jnp.where(k < held, ((h * lo + l) * S + s) * held + k, -2)
        counts = jnp.zeros((tb, LANES), F32)
        start = pl.multiple_of(i * tb, tb)
        for j in range(ngroup):
            lhs, rhs = [], []
            part = resid[:, j * LANES:(j + 1) * LANES]
            for mm in range(group):
                m = j * group + mm
                lhs.append(jnp.where(codes_ref[m:m + 1, :] == code, 1.0, 0.0).astype(BF))
                data = jnp.where(lane // SUB == mm, part.astype(F32), 0.0).astype(BF)
                cnt = jnp.where(lane == m, w_hi, jnp.where(lane == 64 + m, w_lo, 0.0)).astype(BF)
                rhs.append(jnp.concatenate([data, cnt], axis=1))
            out = jnp.dot(jnp.concatenate(lhs, axis=1), jnp.concatenate(rhs, axis=0),
                          preferred_element_type=F32)
            table[pl.ds(start, tb), j * LANES:(j + 1) * LANES] = out[:, :LANES]
            table16[pl.ds(start, tb), j * LANES:(j + 1) * LANES] = out[:, :LANES].astype(BF)
            counts = counts + out[:, LANES:]
        total = counts + pltpu.roll(counts, 64, 1)
        table[pl.ds(start, tb), width:] = total
        table16[pl.ds(start, tb), width:] = split(total)
        return carry

    def split(total):
        first = total.astype(BF)
        keep = lax.broadcasted_iota(I32, total.shape, 1) < 64
        return jnp.where(keep, first.astype(F32), total - first.astype(F32)).astype(BF)

    def joined(block):
        wide = block.astype(F32)
        tail = wide[:, width:]
        return jnp.concatenate([wide[:, :width], tail + pltpu.roll(tail, 64, 1)], axis=1)

    def narrow(block):
        return jnp.concatenate([block[:, :width].astype(BF), split(block[:, width:])], axis=1)

    lax.fori_loop(0, nrow // tb, build, 0)

    n1, n2 = lo * hi * heldp, hi * heldp

    def swap(src, dst, at, device):
        return pltpu.make_async_remote_copy(
            src_ref=src, dst_ref=dst, send_sem=t_s.at[at], recv_sem=t_r.at[at],
            device_id=device, device_id_type=MESH)

    other = 1 - si
    one = swap(table16.at[pl.ds(pl.multiple_of(other * n1, 16), n1)], got1, 0, {"lists": li, "sub": other})
    one.start()
    row_recv, row_sent = exchange(row_send, row_got, row_s, row_r)
    one.wait_recv()
    lo_o = 1 - lo_i
    mine1 = pl.multiple_of(si * n1, 16)
    away = pl.multiple_of(lo_o * n2, 16)
    near = pl.multiple_of(lo_i * n2, 16)
    send2[...] = narrow(table[pl.ds(mine1 + away, n2), :] + joined(got1[pl.ds(away, n2), :]))
    two = swap(send2, got2, 1, {"lists": hi_i * lo + lo_o, "sub": si})
    two.start()
    acc = table[pl.ds(mine1 + near, n2), :] + joined(got1[pl.ds(near, n2), :])
    two.wait_recv()
    acc = acc + joined(got2[...])
    table[0:n2, :] = acc
    send3[...] = narrow(acc).reshape(hi, heldp, width + LANES)

    def third(j, frm):
        return pltpu.make_async_remote_copy(
            src_ref=send3.at[lax.rem(hi_i + j, hi)], dst_ref=got3.at[frm],
            send_sem=t_s.at[2 + j], recv_sem=t_r.at[2 + j],
            device_id={"lists": lax.rem(hi_i + j, hi) * lo + lo_i, "sub": si}, device_id_type=MESH)

    def third_start(j, carry):
        third(j, hi_i).start()
        return carry

    lax.fori_loop(1, hi, third_start, 0)

    def third_recv(j, total):
        frm = lax.rem(hi_i + hi - j, hi)
        third(j, frm).wait_recv()
        return total + joined(got3[frm])

    total = lax.fori_loop(
        1, hi, third_recv, table[pl.ds(pl.multiple_of(hi_i * heldp, heldp), heldp), :])
    row = lax.broadcasted_iota(I32, (LANES, width), 0)
    col = lax.broadcasted_iota(I32, (LANES, width), 1)
    expand = jnp.where((row == col // SUB), 1.0, 0.0).astype(BF)
    inv = 1.0 / jnp.maximum(total[:, width:], 1.0)
    wide = jnp.zeros((heldp, width), F32)
    for _ in range(3):
        top = inv.astype(BF)
        wide = wide + jnp.dot(top, expand, preferred_element_type=F32)
        inv = inv - top.astype(F32)
    code_out[...] = (total[:, :width] * wide)[:held]

    row_recv()
    rows_out[...] = row_got[...].reshape(D * capp, width)

    id_sent()
    cent_sent()
    row_sent()
    one.wait_send()
    two.wait_send()

    def third_sent(j, carry):
        third(j, hi_i).wait_send()
        return carry

    lax.fori_loop(1, hi, third_sent, 0)


def update_kernel(ids_ref, rows_ref, cent_ref, out_ref):
    blk = cent_ref.shape[0]
    n = rows_ref.shape[0]
    base = pl.program_id(0) * blk
    slot = lax.broadcasted_iota(I32, (blk, n), 0) + base
    hit = jnp.where(slot == ids_ref[0:1, :], 1.0, 0.0)
    count = jnp.sum(hit, axis=1, keepdims=True)
    sums = jnp.dot(hit.astype(BF), rows_ref[...], preferred_element_type=F32)
    cent = cent_ref[...].astype(F32)
    out_ref[...] = (cent + (sums - count * cent) * (1.0 / (count + 1.0))).astype(BF)


def shards(tokens, w_in, w_out, gain, centroids, list_slot, assign, codes, list_weight):
    count, length, width = tokens.shape
    parts = codes.shape[1]
    slots_dev = centroids.shape[0]
    L, S = lax.axis_size("lists"), lax.axis_size("sub")
    D = L * S
    lo = 2
    hi = L // lo
    cap = max(2, (2 * count + D - 1) // D)
    capp = up(cap, 16)
    held = CODES // D
    heldp = up(held, 16)
    padded = up(count, LANES)
    ff = w_in.shape[1]
    wtab = width + LANES

    slot = jnp.pad(jnp.take(list_slot, assign), (0, padded - count), constant_values=-1)
    weight = jnp.pad(jnp.take(list_weight, assign), (0, padded - count))
    codes_t = jnp.pad(codes.T, ((0, 0), (0, padded - count)), constant_values=-1)

    cfg = (L, S, lo, hi, cap, capp, slots_dev, held, heldp)
    vm = pl.BlockSpec(memory_space=pltpu.VMEM)
    anyspace = pl.BlockSpec(memory_space=pl.ANY)
    n1, n2 = lo * hi * heldp, hi * heldp
    dma = pltpu.SemaphoreType.DMA
    rows, ids, codewords = pl.pallas_call(
        functools.partial(main_kernel, cfg),
        out_shape=(
            jax.ShapeDtypeStruct((D * capp, width), BF),
            jax.ShapeDtypeStruct((8, D * capp), I32),
            jax.ShapeDtypeStruct((held, width), F32),
        ),
        in_specs=[vm] * 5 + [anyspace] * 4,
        out_specs=(vm, vm, vm),
        scratch_shapes=[
            pltpu.VMEM((count * length, width), BF),
            pltpu.VMEM((width, ff), BF),
            pltpu.VMEM((ff, width), BF),
            pltpu.VMEM((slots_dev, width), BF),
            pltpu.VMEM((padded, width), BF),
            pltpu.VMEM((D, capp, LANES), I32),
            pltpu.VMEM((D, capp, LANES), I32),
            pltpu.VMEM((D, capp, width), BF),
            pltpu.VMEM((D, capp, width), BF),
            pltpu.VMEM((D, capp, width), BF),
            pltpu.VMEM((D, capp, width), BF),
            pltpu.VMEM((S * n1, wtab), F32),
            pltpu.VMEM((S * n1, wtab), BF),
            pltpu.VMEM((n1, wtab), BF),
            pltpu.VMEM((n2, wtab), BF),
            pltpu.VMEM((n2, wtab), BF),
            pltpu.VMEM((hi, heldp, wtab), BF),
            pltpu.VMEM((hi, heldp, wtab), BF),
            dma((16,)),
            dma((D,)), dma((D,)), dma((D,)), dma((D,)), dma((D,)), dma((D,)),
            dma((2 + hi,)), dma((2 + hi,)),
        ],
        compiler_params=pltpu.CompilerParams(
            collective_id=0, has_side_effects=True, vmem_limit_bytes=60 * 1024 * 1024),
        name="encode_route",
    )(
        slot.reshape(1, padded), slot.reshape(padded, 1), weight.reshape(padded, 1), codes_t,
        gain.reshape(1, width), tokens.reshape(count * length, width), w_in, w_out, centroids,
    )

    blk = min(512, slots_dev)
    updated = pl.pallas_call(
        update_kernel,
        grid=(slots_dev // blk,),
        out_shape=jax.ShapeDtypeStruct((slots_dev, width), BF),
        in_specs=[
            pl.BlockSpec((8, D * capp), lambda i: (0, 0)),
            pl.BlockSpec((D * capp, width), lambda i: (0, 0)),
            pl.BlockSpec((blk, width), lambda i: (i, 0)),
        ],
        out_specs=pl.BlockSpec((blk, width), lambda i: (i, 0)),
        compiler_params=pltpu.CompilerParams(vmem_limit_bytes=40 * 1024 * 1024),
        name="update_lists",
    )(ids, rows, centroids)
    return updated, codewords


def solution(mesh):
    return jax.shard_map(
        shards,
        mesh=mesh,
        in_specs=(
            P(("groups", "lists", "sub"), None, None),
            P(),
            P(),
            P(),
            P(("lists", "sub"), None),
            P("groups"),
            P(("groups", "lists", "sub")),
            P(("groups", "lists", "sub"), None),
            P("groups"),
        ),
        out_specs=(P(("groups", "lists", "sub"), None), P(("groups", "lists", "sub"), None)),
        check_vma=False,
    )
```

time: 207 us -> 67.6 us (0.33)
  waiting for transfers between devices: 111 us -> 0 us
  Pallas kernels: 0 us -> 52 us
  matrix products: 35.4 us -> 0 us
  starting transfers between devices: 17.2 us -> 0 us
  between operations: 14.4 us -> 0.67 us
  other arithmetic: 13.8 us -> 2.03 us
  local copies, waits for them, and re-layouts: 15.4 us -> 12.5 us
    reduce_scatter x2 -> x0, waiting for transfers between devices: 103 us -> none  [the longest x1 58.9 us: shards(): lax.psum_scatter(sums, ('lists', 'sub'), scatter_dimension=0, tiled=True)]
    pallas_call x0 -> x2, Pallas kernels: none -> 52 us  [the longest x1 45.2 us: shards(): pl.pallas_call(functools.partial(main_kernel, cfg), out_shape=(jax.ShapeD...]
    dot_general x6 -> x0, matrix products: 35.4 us -> none  [the longest x1 11.2 us: encode(): jnp.dot(hidden, w_out, preferred_element_type=jnp.float32)]
    all_to_all x3 -> x0, starting transfers between devices: 16.9 us -> none  [the longest x1 7.36 us: shards(): lax.all_to_all(id_buf.reshape(devices, row_cap), ('lists', 'sub'), split_...]
    all_to_all x3 -> x0, waiting for transfers between devices: 7.35 us -> none  [the longest x1 4.9 us: shards(): lax.all_to_all(row_buf.reshape(devices, row_cap, width), ('lists', 'sub')...]
    reduce_sum x8 -> x0, other arithmetic: 6.3 us -> none  [the longest x3 3.71 us: step(): counts = counts + jnp.sum(onehot, axis=0).T]
    scatter x2 -> x0, other arithmetic: 2.51 us -> none  [the longest x1 1.66 us: shards(): jnp.zeros((devices * row_cap, width), jnp.bfloat16).at[dest].set(pooled)]
    gather x3 -> x2, local copies, waits for them, and re-layouts: 4.78 us -> 3.03 us  [the longest x1 1.88 us: shards(): jnp.take(list_slot, assign)]
  transfers between devices with their start and end apart: 5 -> 0, of which waited for: 4 -> 0; matrix products, arithmetic and copies ran while one was open for 21% -> 0% of each run, Pallas kernels for 0% -> 0%
where the time goes in v1:
time: 67.6 us; the launch traced here: 67.2 us
  Pallas kernels  52 us (77%)
  local copies, waits for them, and re-layouts  12.5 us (18%)
  other arithmetic  2.03 us (3%)
    pallas_call x1, Pallas kernels, shards(): pl.pallas_call(functools.partial(main_kernel, cfg), out_shape=(jax.ShapeD...  45.2 us
    pallas_call x1, Pallas kernels, shards(): pl.pallas_call(update_kernel, grid=(slots_dev // blk,), out_shape=jax.Sha...  6.8 us
    unnamed x11, local copies, waits for them, and re-layouts  6 us
    gather x1, local copies, waits for them, and re-layouts, shards(): jnp.take(list_slot, assign)  1.88 us
    pad x1, local copies, waits for them, and re-layouts, shards(): jnp.pad(codes.T, ((0, 0), (0, padded - count)), constant_values=-1)  1.37 us
    select_n x2, other arithmetic, shards(): jnp.take(list_slot, assign)  1.36 us

profile of v1, /device:TPU:0, one launch (start us, length us, event | category | flops | bytes accessed | tf_op | source)
XLA Modules:
  0.0 67.2 jit_solution(11360666372318507311)
XLA Ops:
  0.6 0.0 copy-start
  0.6 0.7 %compare_select_fusion = s32[96]{0:T(128)S(1)} fusion(s32[96]{0:T(128)} %param.15), kind=kLoop, calls=%fused_computation.3 | loop fusion | flops 288 | bytes 768 | tf_op jit(solution)/shard_map/jit(_take)/jit(_where)/select_n | solution.py:332
  1.4 0.2 copy-done
  1.6 1.1 %gather_fusion.1 = f32[96]{0:T(128)S(1)} fusion(f32[65536]{0:T(1024)S(1)} %copy-done, s32[1024]{0:T(1024)S(1)} %pad_clamp_fusion), kind=kCustom, calls=%fused_computation.1 | custom fusion | bytes 1152 | tf_op jit(solution)/shard_map/jit(_take)/gather | solution.py:333
  2.8 1.9 %gather_fusion = s32[96]{0:T(128)S(1)} fusion(s32[65536]{0:T(1024)} %param.14, s32[1024]{0:T(1024)S(1)} %pad_clamp_fusion), kind=kCustom, calls=%fused_computation | custom fusion | bytes 1152 | tf_op jit(solution)/shard_map/jit(_take)/gather | solution.py:332
  4.6 0.7 broadcast_select_fusion.1
  5.3 0.7 broadcast_select_fusion
  6.0 0.6 pad_bitcast_fusion.1
  6.5 1.4 %pad.14.codes_ref = s32[64,128]{1,0:T(8,128)} pad(s32[64,96]{1,0:T(8,128)} %bitcast.10, s32[]{:T(128)} %constant.31.clone.1), padding=0_0x0_32 | pad | bytes 57348 | tf_op jit(solution)/shard_map/jit(_pad)/pad | solution.py:334
  7.9 0.7 %copy.13.slot_col_ref = s32[128,1]{1,0:T(8,128)} copy(s32[128,1]{0,1:T(1,128)S(1)} %get-tuple-element.8) | data formatting | bytes 1024 | tf_op jit(solution)/shard_map/reshape | solution.py:377
  8.6 0.7 %copy.14.weight_ref = f32[128,1]{1,0:T(8,128)} copy(f32[128,1]{0,1:T(1,128)S(1)} %pad_bitcast_fusion) | data formatting | bytes 1024 | tf_op jit(solution)/shard_map/reshape | solution.py:377
  9.4 45.2 %encode_route.1 = (bf16[256,1024]{1,0:T(8,128)(2,1)}, s32[8,256]{1,0:T(8,128)}, f32[16,1024]{1,0:T(8,128)}) custom-call(s32[1,128]{1,0:T(1,128)} %get-tuple-element.9.slot_row_ref, s32[128,1]{1,0:T(8,128)} %copy.13.slot_col_ref, f32[128,1]{1,0:T(8,128)} %copy.14.weight_ref, s32[64,128]{1,0:T(8,128)} %pad.14.codes_ref, f32[1,1024]{1,0:T(1,128)} %bitcast.11, ...), custom_call_target="tpu_custom_call" | custom-call | tf_op jit(solution)/shard_map/encode_route/pallas_call | solution.py:341
  54.6 0.0 copy-start.1
  54.6 3.4 %copy-done.1 = bf16[4096,1024]{1,0:T(8,128)(2,1)S(1)} copy-done((bf16[4096,1024]{1,0:T(8,128)(2,1)S(1)}, bf16[4096,1024]{1,0:T(8,128)(2,1)}, u32[]{:S(2)}) %copy-start.1) | copy-done | bytes 8388632
  58.0 0.0 copy-start.2
  58.0 1.0 %copy-done.2 = bf16[256,1024]{1,0:T(8,128)(2,1)S(1)} copy-done((bf16[256,1024]{1,0:T(8,128)(2,1)S(1)}, bf16[256,1024]{1,0:T(8,128)(2,1)}, u32[]{:S(2)}) %copy-start.2) | copy-done | bytes 524312
  59.0 0.0 copy-start.3
  59.0 0.7 %copy-done.3 = s32[8,256]{1,0:T(8,128)S(1)} copy-done((s32[8,256]{1,0:T(8,128)S(1)}, s32[8,256]{1,0:T(8,128)}, u32[]{:S(2)}) %copy-start.3) | copy-done | bytes 8216
  59.7 0.0 copy-start.4
  59.7 6.8 %update_lists.1 = bf16[4096,1024]{1,0:T(8,128)(2,1)} custom-call(s32[8,256]{1,0:T(8,128)S(1)} %copy-done.3, bf16[256,1024]{1,0:T(8,128)(2,1)S(1)} %copy-done.2, bf16[4096,1024]{1,0:T(8,128)(2,1)S(1)} %copy-done.1), custom_call_target="tpu_custom_call" | custom-call | tf_op jit(solution)/shard_map/update_lists/pallas_call | solution.py:382
  66.5 0.0 copy-done.4
  66.5 0.6 copy.16
  (2 shorter events, 0.0 us)
Async XLA Ops:
  0.6 1.0 %copy-start = (f32[65536]{0:T(1024)S(1)}, f32[65536]{0:T(1024)}, u32[]{:S(2)}) copy-start(f32[65536]{0:T(1024)} %param.17) | copy-start | bytes 786436
  54.6 3.4 %copy-start.1 = (bf16[4096,1024]{1,0:T(8,128)(2,1)S(1)}, bf16[4096,1024]{1,0:T(8,128)(2,1)}, u32[]{:S(2)}) copy-start(bf16[4096,1024]{1,0:T(8,128)(2,1)} %cent_ref.1) | copy-start | bytes 25165828
  58.0 1.0 %copy-start.2 = (bf16[256,1024]{1,0:T(8,128)(2,1)S(1)}, bf16[256,1024]{1,0:T(8,128)(2,1)}, u32[]{:S(2)}) copy-start(bf16[256,1024]{1,0:T(8,128)(2,1)} %get-tuple-element.6.rows_ref) | copy-start | bytes 1572868
  59.0 0.7 %copy-start.3 = (s32[8,256]{1,0:T(8,128)S(1)}, s32[8,256]{1,0:T(8,128)}, u32[]{:S(2)}) copy-start(s32[8,256]{1,0:T(8,128)} %get-tuple-element.5.ids_ref) | copy-start | bytes 24580
  59.7 6.8 %copy-start.4 = (f32[16,1024]{1,0:T(8,128)S(1)}, f32[16,1024]{1,0:T(8,128)}, u32[]{:S(2)}) copy-start(f32[16,1024]{1,0:T(8,128)} %get-tuple-element.13) | copy-start | bytes 196612

commit v2 on v1

--- a/solution.py
+++ b/solution.py
@@ -25,19 +25,20 @@
 
 def main_kernel(
     cfg,
-    slot_row_ref, slot_col_ref, weight_ref, codes_ref, gain_ref,
+    assign_ref, codes_in, gain_ref, slot_hbm, weight_hbm,
     tok_hbm, win_hbm, wout_hbm, cent_hbm,
     rows_out, ids_out, code_out,
+    slot_tab, weight_tab, slot_hit, weight_hit, codes_pad, codes_ref,
     tok, win, wout, cent, pooled,
     ids_send, ids_got, cent_send, cent_got, row_send, row_got,
-    table, table16, got1, send2, got2, send3, got3,
+    table, acc3, got1, send2, got2, send3, got3,
     load_sem, id_s, id_r, cent_s, cent_r, row_s, row_r, t_s, t_r,
 ):
     L, S, lo, hi, cap, capp, slots_dev, held, heldp = cfg
     D = L * S
     width = tok.shape[1]
     passages = tok.shape[0] // 8
-    padded = slot_row_ref.shape[1]
+    padded = slot_hit.shape[0]
     li, si = lax.axis_index("lists"), lax.axis_index("sub")
     me = li * S + si
     hi_i, lo_i = li // lo, lax.rem(li, lo)
@@ -55,9 +56,13 @@
         loads.append(pltpu.make_async_copy(
             wout_hbm.at[pl.ds(c * fc, fc), :], wout.at[pl.ds(c * fc, fc), :], load_sem.at[2 + 2 * c]))
     cent_load = pltpu.make_async_copy(cent_hbm, cent, load_sem.at[1 + 2 * nchunk])
+    slot_load = pltpu.make_async_copy(slot_hbm, slot_tab, load_sem.at[2 + 2 * nchunk])
+    weight_load = pltpu.make_async_copy(weight_hbm, weight_tab, load_sem.at[3 + 2 * nchunk])
+    slot_load.start()
+    weight_load.start()
+    cent_load.start()
     for one in loads:
         one.start()
-    cent_load.start()
 
     barrier = pltpu.get_barrier_semaphore()
 
@@ -68,11 +73,29 @@
     lax.fori_loop(1, D, greet, 0)
 
     shift = slots_dev.bit_length() - 1
-    slot_row, slot_col = slot_row_ref[...], slot_col_ref[...]
+    slot_hit[...] = jnp.zeros_like(slot_hit)
+    weight_hit[...] = jnp.zeros_like(weight_hit)
+    lane1 = lax.broadcasted_iota(I32, (1, LANES), 1)
+    slot_load.wait()
+    weight_load.wait()
+
+    def look(p, carry):
+        a = assign_ref[p]
+        row = lax.shift_right_logical(a, 7)
+        at = lane1 == jnp.bitwise_and(a, LANES - 1)
+        slot_hit[pl.ds(p, 1), :] = jnp.where(at, slot_tab[pl.ds(row, 1), :].astype(F32), 0.0)
+        weight_hit[pl.ds(p, 1), :] = jnp.where(at, weight_tab[pl.ds(row, 1), :], 0.0)
+        return carry
+
+    lax.fori_loop(0, passages, look, 0, unroll=8)
+    below = lax.broadcasted_iota(I32, (padded, 1), 0) < passages
+    slot_f = jnp.where(below, jnp.sum(slot_hit[...], axis=1, keepdims=True), -1.0)
+    slot_col = slot_f.astype(I32)
+    i0 = lax.broadcasted_iota(I32, (padded, padded), 0)
+    i1 = lax.broadcasted_iota(I32, (padded, padded), 1)
+    slot_row = jnp.sum(jnp.where(i0 == i1, slot_f, 0.0), axis=0, keepdims=True).astype(I32)
     tr = jnp.where(slot_row >= 0, lax.shift_right_logical(slot_row, shift), -1)
     tc = jnp.where(slot_col >= 0, lax.shift_right_logical(slot_col, shift), -1)
-    i0 = lax.broadcasted_iota(I32, (padded, padded), 0)
-    i1 = lax.broadcasted_iota(I32, (padded, padded), 1)
     same = tr == tc
     rank_row = jnp.sum(jnp.where(same & (i0 < i1), 1.0, 0.0), axis=0, keepdims=True).astype(I32)
     rank_col = jnp.sum(jnp.where(same & (i1 < i0), 1.0, 0.0), axis=1, keepdims=True).astype(I32)
@@ -140,10 +163,6 @@
         scale = lax.rsqrt(jnp.mean(avg * avg, axis=-1, keepdims=True) + 1e-06)
         pooled[pl.ds(b * per, per), :] = (avg * scale).astype(BF)
 
-    pooled[...] = jnp.zeros_like(pooled)
-    loads[0].wait()
-    encode(0, True)
-
     id_recv()
     cent_load.wait()
     want = ids_got[...].reshape(D * capp, LANES)
@@ -162,19 +181,28 @@
     cent_got[me] = cent_send[me]
     cent_recv, cent_sent = exchange(cent_send, cent_got, cent_s, cent_r)
 
-    for b in range(1, nblk):
-        encode(b, False)
+    codes_pad[...] = jnp.full(codes_pad.shape, -1.0, F32)
+    codes_pad[0:passages, 0:codes_in.shape[1]] = codes_in[...].astype(F32)
+    codes_ref[...] = codes_pad[...].T
+
+    pooled[...] = jnp.zeros_like(pooled)
+    loads[0].wait()
+    for b in range(nblk):
+        encode(b, b == 0)
 
     put = jnp.where(spread, 1.0, 0.0).astype(BF)
     row_send[...] = jnp.dot(put, pooled[...], preferred_element_type=F32).astype(BF).reshape(D, capp, width)
     row_got[me] = row_send[me]
+    row_recv, row_sent = exchange(row_send, row_got, row_s, row_r)
 
     cent_recv()
     get = jnp.where(
         lax.broadcasted_iota(I32, (padded, D * capp), 1) == dest_col, 1.0, 0.0).astype(BF)
     cent_rows = jnp.dot(get, cent_got[...].reshape(D * capp, width), preferred_element_type=F32)
-    weight = weight_ref[...]
-    resid = ((pooled[...].astype(F32) - cent_rows) * weight).astype(BF)
+    weight = jnp.sum(weight_hit[...], axis=1, keepdims=True)
+    resid = (pooled[...].astype(F32) - cent_rows) * weight
+    r_hi = resid.astype(BF).astype(F32)
+    r_lo = resid - r_hi
     w_hi = weight.astype(BF).astype(F32)
     w_lo = weight - w_hi
 
@@ -193,26 +221,28 @@
         rest = lax.shift_right_logical(rest, hi.bit_length() - 1)
         l = jnp.bitwise_and(rest, lo - 1)
         s = lax.shift_right_logical(rest, lo.bit_length() - 1)
-        code = jnp.where(k < held, ((h * lo + l) * S + s) * held + k, -2)
+        code = jnp.where(k < held, ((h * lo + l) * S + s) * held + k, -2).astype(F32)
         counts = jnp.zeros((tb, LANES), F32)
         start = pl.multiple_of(i * tb, tb)
         for j in range(ngroup):
             lhs, rhs = [], []
-            part = resid[:, j * LANES:(j + 1) * LANES]
+            part_hi = r_hi[:, j * LANES:(j + 1) * LANES]
+            part_lo = r_lo[:, j * LANES:(j + 1) * LANES]
             for mm in range(group):
                 m = j * group + mm
                 lhs.append(jnp.where(codes_ref[m:m + 1, :] == code, 1.0, 0.0).astype(BF))
-                data = jnp.where(lane // SUB == mm, part.astype(F32), 0.0).astype(BF)
+                own = lane // SUB == mm
+                data = jnp.where(own, part_hi, 0.0).astype(BF)
+                rest_data = jnp.where(own, part_lo, 0.0).astype(BF)
                 cnt = jnp.where(lane == m, w_hi, jnp.where(lane == 64 + m, w_lo, 0.0)).astype(BF)
-                rhs.append(jnp.concatenate([data, cnt], axis=1))
+                rhs.append(jnp.concatenate([data, rest_data, cnt], axis=1))
             out = jnp.dot(jnp.concatenate(lhs, axis=1), jnp.concatenate(rhs, axis=0),
                           preferred_element_type=F32)
-            table[pl.ds(start, tb), j * LANES:(j + 1) * LANES] = out[:, :LANES]
-            table16[pl.ds(start, tb), j * LANES:(j + 1) * LANES] = out[:, :LANES].astype(BF)
-            counts = counts + out[:, LANES:]
+            table[pl.ds(start, tb), j * LANES:(j + 1) * LANES] = (
+                out[:, :LANES] + out[:, LANES:2 * LANES])
+            counts = counts + out[:, 2 * LANES:]
         total = counts + pltpu.roll(counts, 64, 1)
         table[pl.ds(start, tb), width:] = total
-        table16[pl.ds(start, tb), width:] = split(total)
         return carry
 
     def split(total):
@@ -238,21 +268,20 @@
             device_id=device, device_id_type=MESH)
 
     other = 1 - si
-    one = swap(table16.at[pl.ds(pl.multiple_of(other * n1, 16), n1)], got1, 0, {"lists": li, "sub": other})
+    one = swap(table.at[pl.ds(pl.multiple_of(other * n1, 16), n1)], got1, 0, {"lists": li, "sub": other})
     one.start()
-    row_recv, row_sent = exchange(row_send, row_got, row_s, row_r)
     one.wait_recv()
     lo_o = 1 - lo_i
     mine1 = pl.multiple_of(si * n1, 16)
     away = pl.multiple_of(lo_o * n2, 16)
     near = pl.multiple_of(lo_i * n2, 16)
-    send2[...] = narrow(table[pl.ds(mine1 + away, n2), :] + joined(got1[pl.ds(away, n2), :]))
+    send2[...] = narrow(table[pl.ds(mine1 + away, n2), :] + got1[pl.ds(away, n2), :])
     two = swap(send2, got2, 1, {"lists": hi_i * lo + lo_o, "sub": si})
     two.start()
-    acc = table[pl.ds(mine1 + near, n2), :] + joined(got1[pl.ds(near, n2), :])
+    acc = table[pl.ds(mine1 + near, n2), :] + got1[pl.ds(near, n2), :]
     two.wait_recv()
     acc = acc + joined(got2[...])
-    table[0:n2, :] = acc
+    acc3[...] = acc.reshape(hi, heldp, width + LANES)
     send3[...] = narrow(acc).reshape(hi, heldp, width + LANES)
 
     def third(j, frm):
@@ -273,7 +302,7 @@
         return total + joined(got3[frm])
 
     total = lax.fori_loop(
-        1, hi, third_recv, table[pl.ds(pl.multiple_of(hi_i * heldp, heldp), heldp), :])
+        1, hi, third_recv, acc3[hi_i])
     row = lax.broadcasted_iota(I32, (LANES, width), 0)
     col = lax.broadcasted_iota(I32, (LANES, width), 1)
     expand = jnp.where((row == col // SUB), 1.0, 0.0).astype(BF)
@@ -315,7 +344,6 @@
 
 def shards(tokens, w_in, w_out, gain, centroids, list_slot, assign, codes, list_weight):
     count, length, width = tokens.shape
-    parts = codes.shape[1]
     slots_dev = centroids.shape[0]
     L, S = lax.axis_size("lists"), lax.axis_size("sub")
     D = L * S
@@ -329,10 +357,6 @@
     ff = w_in.shape[1]
     wtab = width + LANES
 
-    slot = jnp.pad(jnp.take(list_slot, assign), (0, padded - count), constant_values=-1)
-    weight = jnp.pad(jnp.take(list_weight, assign), (0, padded - count))
-    codes_t = jnp.pad(codes.T, ((0, 0), (0, padded - count)), constant_values=-1)
-
     cfg = (L, S, lo, hi, cap, capp, slots_dev, held, heldp)
     vm = pl.BlockSpec(memory_space=pltpu.VMEM)
     anyspace = pl.BlockSpec(memory_space=pl.ANY)
@@ -345,9 +369,15 @@
             jax.ShapeDtypeStruct((8, D * capp), I32),
             jax.ShapeDtypeStruct((held, width), F32),
         ),
-        in_specs=[vm] * 5 + [anyspace] * 4,
+        in_specs=[pl.BlockSpec(memory_space=pltpu.SMEM)] + [vm] * 2 + [anyspace] * 6,
         out_specs=(vm, vm, vm),
         scratch_shapes=[
+            pltpu.VMEM((list_slot.shape[0] // LANES, LANES), I32),
+            pltpu.VMEM((list_slot.shape[0] // LANES, LANES), F32),
+            pltpu.VMEM((padded, LANES), F32),
+            pltpu.VMEM((padded, LANES), F32),
+            pltpu.VMEM((padded, LANES), F32),
+            pltpu.VMEM((LANES, padded), F32),
             pltpu.VMEM((count * length, width), BF),
             pltpu.VMEM((width, ff), BF),
             pltpu.VMEM((ff, width), BF),
@@ -360,8 +390,8 @@
             pltpu.VMEM((D, capp, width), BF),
             pltpu.VMEM((D, capp, width), BF),
             pltpu.VMEM((S * n1, wtab), F32),
-            pltpu.VMEM((S * n1, wtab), BF),
-            pltpu.VMEM((n1, wtab), BF),
+            pltpu.VMEM((hi, heldp, wtab), F32),
+            pltpu.VMEM((n1, wtab), F32),
             pltpu.VMEM((n2, wtab), BF),
             pltpu.VMEM((n2, wtab), BF),
             pltpu.VMEM((hi, heldp, wtab), BF),
@@ -374,8 +404,8 @@
             collective_id=0, has_side_effects=True, vmem_limit_bytes=60 * 1024 * 1024),
         name="encode_route",
     )(
-        slot.reshape(1, padded), slot.reshape(padded, 1), weight.reshape(padded, 1), codes_t,
-        gain.reshape(1, width), tokens.reshape(count * length, width), w_in, w_out, centroids,
+        assign, codes, gain.reshape(1, width),
+        list_slot.reshape(-1, LANES), list_weight.reshape(-1, LANES), tokens.reshape(count * length, width), w_in, w_out, centroids,
     )
 
     blk = min(512, slots_dev)
@@ -389,7 +419,7 @@
             pl.BlockSpec((blk, width), lambda i: (i, 0)),
         ],
         out_specs=pl.BlockSpec((blk, width), lambda i: (i, 0)),
-        compiler_params=pltpu.CompilerParams(vmem_limit_bytes=40 * 1024 * 1024),
+        compiler_params=pltpu.CompilerParams(vmem_limit_bytes=62 * 1024 * 1024),
         name="update_lists",
     )(ids, rows, centroids)
     return updated, codewords

time: 67.6 us -> 61.3 us (0.907)
  local copies, waits for them, and re-layouts: 12.5 us -> 2.1 us
  Pallas kernels: 52 us -> 58.1 us
  other arithmetic: 2.03 us -> 0 us
    pallas_call x1, Pallas kernels: 6.8 us -> 10.9 us  [shards(): pl.pallas_call(update_kernel, grid=(slots_dev // blk,), out_shape=jax.Sha...]
    unnamed x11 -> x4, local copies, waits for them, and re-layouts: 6 us -> 2.1 us
    gather x2 -> x0, local copies, waits for them, and re-layouts: 3.03 us -> none  [the longest x1 1.88 us: shards(): jnp.take(list_slot, assign)]
    reshape x4 -> x0, local copies, waits for them, and re-layouts: 2.06 us -> none  [the longest x2 1.32 us: shards(): slot.reshape(padded, 1)]
    pallas_call x1, Pallas kernels: 45.2 us -> 47.2 us  [shards(): pl.pallas_call(functools.partial(main_kernel, cfg), out_shape=(jax.ShapeD...]
    select_n x3 -> x0, other arithmetic: 2.02 us -> none  [the longest x2 1.36 us: shards(): jnp.take(list_slot, assign)]
    pad x1 -> x0, local copies, waits for them, and re-layouts: 1.37 us -> none  [shards(): jnp.pad(codes.T, ((0, 0), (0, padded - count)), constant_values=-1)]
where the time goes in v2:
time: 61.3 us; the launch traced here: 60.9 us
  Pallas kernels  58.1 us (95%)
  local copies, waits for them, and re-layouts  2.1 us (3%)
  between operations  0.65 us (1%)
    pallas_call x1, Pallas kernels, shards(): pl.pallas_call(functools.partial(main_kernel, cfg), out_shape=(jax.ShapeD...  47.2 us
    pallas_call x1, Pallas kernels, shards(): pl.pallas_call(update_kernel, grid=(slots_dev // blk,), out_shape=jax.Sha...  10.9 us
    unnamed x4, local copies, waits for them, and re-layouts  2.1 us

profile of v2, /device:TPU:0, one launch (start us, length us, event | category | flops | bytes accessed | tf_op | source)
XLA Modules:
  0.0 60.9 jit_solution(16730792020160011437)
XLA Ops:
  0.6 1.5 %copy.11.codes_in = s32[96,64]{1,0:T(8,128)} copy(s32[96,64]{0,1:T(8,128)} %param.16) | data formatting | bytes 49152 | tf_op args[7]
  2.1 47.2 %encode_route.1 = (bf16[256,1024]{1,0:T(8,128)(2,1)}, s32[8,256]{1,0:T(8,128)}, f32[16,1024]{1,0:T(8,128)}) custom-call(s32[96]{0:T(128)} %assign_ref.1, s32[96,64]{1,0:T(8,128)} %copy.11.codes_in, f32[1,1024]{1,0:T(1,128)} %bitcast.7, s32[512,128]{1,0:T(8,128)} %bitcast.5, f32[512,128]{1,0:T(8,128)} %bitcast.6, bf16[768,1024]{1,0:T(8,128)(2,1)} %bitcast.4, ...), custom_call_target="tpu_custom_call" | custom-call | tf_op jit(solution)/shard_map/encode_route/pallas_call | solution.py:365
  49.3 0.0 copy-start
  49.4 10.9 %update_lists.1 = bf16[4096,1024]{1,0:T(8,128)(2,1)} custom-call(s32[8,256]{1,0:T(8,128)} %get-tuple-element.5.ids_ref, bf16[256,1024]{1,0:T(8,128)(2,1)} %get-tuple-element.6.rows_ref, bf16[4096,1024]{1,0:T(8,128)(2,1)} %cent_ref.1), custom_call_target="tpu_custom_call" | custom-call | tf_op jit(solution)/shard_map/update_lists/pallas_call | solution.py:412
  60.3 0.0 copy-done
  60.3 0.6 %copy.13 = f32[16,1024]{1,0:T(8,128)} copy(f32[16,1024]{1,0:T(8,128)S(1)} %copy-done) | data formatting | bytes 131072
Async XLA Ops:
  49.3 10.9 %copy-start = (f32[16,1024]{1,0:T(8,128)S(1)}, f32[16,1024]{1,0:T(8,128)}, u32[]{:S(2)}) copy-start(f32[16,1024]{1,0:T(8,128)} %get-tuple-element.11) | copy-start | bytes 196612

commit v3 on v2

--- a/solution.py
+++ b/solution.py
@@ -34,9 +34,10 @@
     table, acc3, got1, send2, got2, send3, got3,
     load_sem, id_s, id_r, cent_s, cent_r, row_s, row_r, t_s, t_r,
 ):
-    L, S, lo, hi, cap, capp, slots_dev, held, heldp = cfg
+    L, S, lo, hi, cap, capp, cuts, slots_dev, held, heldp = cfg
     D = L * S
     width = tok.shape[1]
+    wq, qc = width // cuts, cuts * cap
     passages = tok.shape[0] // 8
     padded = slot_hit.shape[0]
     li, si = lax.axis_index("lists"), lax.axis_index("sub")
@@ -100,7 +101,8 @@
     rank_row = jnp.sum(jnp.where(same & (i0 < i1), 1.0, 0.0), axis=0, keepdims=True).astype(I32)
     rank_col = jnp.sum(jnp.where(same & (i1 < i0), 1.0, 0.0), axis=1, keepdims=True).astype(I32)
     dest_row = jnp.where(tr >= 0, tr * capp + rank_row, -1)
-    dest_col = jnp.where(tc >= 0, tc * capp + rank_col, -1)
+    packed_row = jnp.where(tr >= 0, tr * qc + rank_row, -(1 << 20))
+    packed_col = jnp.where(tc >= 0, tc * qc + rank_col, -(1 << 20))
     local_row = (slot_row - jnp.maximum(tr, 0) * slots_dev + 1).astype(F32)
     di = lax.broadcasted_iota(I32, (D * capp, padded), 0)
     spread = di == dest_row
@@ -168,13 +170,28 @@
     want = ids_got[...].reshape(D * capp, LANES)
     ids_out[...] = want.T[0:8, :]
     rb = 256
+    rblk = rb // capp
+    cbits = capp.bit_length() - 1
+
+    def stacked(rows):
+        return jnp.concatenate([rows[:, q * wq:(q + 1) * wq] for q in range(cuts)], axis=0)
+
+    def place(index, q):
+        r = jnp.bitwise_and(index, capp - 1)
+        d = lax.shift_right_logical(index, cbits)
+        return jnp.where(r < cap, d * qc + q * cap + r, -1)
+
+    index_row = lax.broadcasted_iota(I32, (1, rb), 1)
+    index_col = lax.broadcasted_iota(I32, (rb, 1), 0)
+    pack = jnp.concatenate([place(index_row, q) for q in range(cuts)], axis=1)
+    pack = jnp.where(lax.broadcasted_iota(I32, (rblk * qc, cuts * rb), 0) == pack, 1.0, 0.0).astype(BF)
 
     def pick(i, carry):
-        start = pl.multiple_of(i * rb, rb)
-        mine = ids_got[pl.ds(i * (rb // capp), rb // capp)].reshape(rb, LANES)[:, 0:1]
+        mine = ids_got[pl.ds(i * rblk, rblk)].reshape(rb, LANES)[:, 0:1]
         hit = jnp.where(lax.broadcasted_iota(I32, (rb, slots_dev), 1) == mine, 1.0, 0.0).astype(BF)
         out = jnp.dot(hit, cent[...], preferred_element_type=F32).astype(BF)
-        cent_send[pl.ds(i * (rb // capp), rb // capp)] = out.reshape(rb // capp, capp, width)
+        out = jnp.dot(pack, stacked(out), preferred_element_type=F32).astype(BF)
+        cent_send[pl.ds(i * rblk, rblk)] = out.reshape(rblk, qc, wq)
         return carry
 
     lax.fori_loop(0, D * capp // rb, pick, 0)
@@ -190,15 +207,20 @@
     for b in range(nblk):
         encode(b, b == 0)
 
-    put = jnp.where(spread, 1.0, 0.0).astype(BF)
-    row_send[...] = jnp.dot(put, pooled[...], preferred_element_type=F32).astype(BF).reshape(D, capp, width)
+    put = jnp.concatenate([packed_row + q * cap for q in range(cuts)], axis=1)
+    put = jnp.where(
+        lax.broadcasted_iota(I32, (D * qc, cuts * padded), 0) == put, 1.0, 0.0).astype(BF)
+    row_send[...] = jnp.dot(
+        put, stacked(pooled[...]), preferred_element_type=F32).astype(BF).reshape(D, qc, wq)
     row_got[me] = row_send[me]
     row_recv, row_sent = exchange(row_send, row_got, row_s, row_r)
 
     cent_recv()
-    get = jnp.where(
-        lax.broadcasted_iota(I32, (padded, D * capp), 1) == dest_col, 1.0, 0.0).astype(BF)
-    cent_rows = jnp.dot(get, cent_got[...].reshape(D * capp, width), preferred_element_type=F32)
+    got_flat = cent_got[...].reshape(D * qc, wq)
+    get_at = lax.broadcasted_iota(I32, (padded, D * qc), 1)
+    cent_rows = jnp.concatenate([
+        jnp.dot(jnp.where(get_at == packed_col + q * cap, 1.0, 0.0).astype(BF), got_flat,
+                preferred_element_type=F32) for q in range(cuts)], axis=1)
     weight = jnp.sum(weight_hit[...], axis=1, keepdims=True)
     resid = (pooled[...].astype(F32) - cent_rows) * weight
     r_hi = resid.astype(BF).astype(F32)
@@ -315,7 +337,18 @@
     code_out[...] = (total[:, :width] * wide)[:held]
 
     row_recv()
-    rows_out[...] = row_got[...].reshape(D * capp, width)
+    flat_at = lax.broadcasted_iota(I32, (rb, rblk * qc), 1)
+
+    def unpack(i, carry):
+        flat = row_got[pl.ds(i * rblk, rblk)].reshape(rblk * qc, wq)
+        start = pl.multiple_of(i * rb, rb)
+        for q in range(cuts):
+            take = jnp.where(flat_at == place(index_col, q), 1.0, 0.0).astype(BF)
+            rows_out[pl.ds(start, rb), q * wq:(q + 1) * wq] = jnp.dot(
+                take, flat, preferred_element_type=F32).astype(BF)
+        return carry
+
+    lax.fori_loop(0, D * capp // rb, unpack, 0)
 
     id_sent()
     cent_sent()
@@ -339,7 +372,7 @@
     count = jnp.sum(hit, axis=1, keepdims=True)
     sums = jnp.dot(hit.astype(BF), rows_ref[...], preferred_element_type=F32)
     cent = cent_ref[...].astype(F32)
-    out_ref[...] = (cent + (sums - count * cent) * (1.0 / (count + 1.0))).astype(BF)
+    out_ref[...] = ((cent + sums) * (1.0 / (count + 1.0))).astype(BF)
 
 
 def shards(tokens, w_in, w_out, gain, centroids, list_slot, assign, codes, list_weight):
@@ -357,7 +390,8 @@
     ff = w_in.shape[1]
     wtab = width + LANES
 
-    cfg = (L, S, lo, hi, cap, capp, slots_dev, held, heldp)
+    cuts = 4 if (4 * cap) % 16 == 0 else 8
+    cfg = (L, S, lo, hi, cap, capp, cuts, slots_dev, held, heldp)
     vm = pl.BlockSpec(memory_space=pltpu.VMEM)
     anyspace = pl.BlockSpec(memory_space=pl.ANY)
     n1, n2 = lo * hi * heldp, hi * heldp
@@ -385,10 +419,10 @@
             pltpu.VMEM((padded, width), BF),
             pltpu.VMEM((D, capp, LANES), I32),
             pltpu.VMEM((D, capp, LANES), I32),
-            pltpu.VMEM((D, capp, width), BF),
-            pltpu.VMEM((D, capp, width), BF),
-            pltpu.VMEM((D, capp, width), BF),
-            pltpu.VMEM((D, capp, width), BF),
+            pltpu.VMEM((D, cuts * cap, width // cuts), BF),
+            pltpu.VMEM((D, cuts * cap, width // cuts), BF),
+            pltpu.VMEM((D, cuts * cap, width // cuts), BF),
+            pltpu.VMEM((D, cuts * cap, width // cuts), BF),
             pltpu.VMEM((S * n1, wtab), F32),
             pltpu.VMEM((hi, heldp, wtab), F32),
             pltpu.VMEM((n1, wtab), F32),

time: 61.3 us -> 60.5 us (0.987)
  Pallas kernels: 58.1 us -> 57.3 us
where the time goes in v3:
time: 60.5 us; the launch traced here: 60.1 us
  Pallas kernels  57.3 us (95%)
  local copies, waits for them, and re-layouts  2.1 us (3%)
  between operations  0.65 us (1%)
    pallas_call x1, Pallas kernels, shards(): pl.pallas_call(functools.partial(main_kernel, cfg), out_shape=(jax.ShapeD...  46.7 us
    pallas_call x1, Pallas kernels, shards(): pl.pallas_call(update_kernel, grid=(slots_dev // blk,), out_shape=jax.Sha...  10.7 us
    unnamed x4, local copies, waits for them, and re-layouts  2.1 us

profile of v3, /device:TPU:0, one launch (start us, length us, event | category | flops | bytes accessed | tf_op | source)
XLA Modules:
  0.0 60.1 jit_solution(8541860258172777254)
XLA Ops:
  0.6 1.5 %copy.11.codes_in = s32[96,64]{1,0:T(8,128)} copy(s32[96,64]{0,1:T(8,128)} %param.16) | data formatting | bytes 49152 | tf_op args[7]
  2.1 46.7 %encode_route.1 = (bf16[256,1024]{1,0:T(8,128)(2,1)}, s32[8,256]{1,0:T(8,128)}, f32[16,1024]{1,0:T(8,128)}) custom-call(s32[96]{0:T(128)} %assign_ref.1, s32[96,64]{1,0:T(8,128)} %copy.11.codes_in, f32[1,1024]{1,0:T(1,128)} %bitcast.7, s32[512,128]{1,0:T(8,128)} %bitcast.5, f32[512,128]{1,0:T(8,128)} %bitcast.6, bf16[768,1024]{1,0:T(8,128)(2,1)} %bitcast.4, ...), custom_call_target="tpu_custom_call" | custom-call | tf_op jit(solution)/shard_map/encode_route/pallas_call | solution.py:399
  48.8 0.0 copy-start
  48.8 10.7 %update_lists.1 = bf16[4096,1024]{1,0:T(8,128)(2,1)} custom-call(s32[8,256]{1,0:T(8,128)} %get-tuple-element.5.ids_ref, bf16[256,1024]{1,0:T(8,128)(2,1)} %get-tuple-element.6.rows_ref, bf16[4096,1024]{1,0:T(8,128)(2,1)} %cent_ref.1), custom_call_target="tpu_custom_call" | custom-call | tf_op jit(solution)/shard_map/update_lists/pallas_call | solution.py:446
  59.4 0.0 copy-done
  59.4 0.6 %copy.13 = f32[16,1024]{1,0:T(8,128)} copy(f32[16,1024]{1,0:T(8,128)S(1)} %copy-done) | data formatting | bytes 131072
Async XLA Ops:
  48.8 10.7 %copy-start = (f32[16,1024]{1,0:T(8,128)S(1)}, f32[16,1024]{1,0:T(8,128)}, u32[]{:S(2)}) copy-start(f32[16,1024]{1,0:T(8,128)} %get-tuple-element.11) | copy-start | bytes 196612

commit v4 on v3

--- a/solution.py
+++ b/solution.py
@@ -28,7 +28,7 @@
     assign_ref, codes_in, gain_ref, slot_hbm, weight_hbm,
     tok_hbm, win_hbm, wout_hbm, cent_hbm,
     rows_out, ids_out, code_out,
-    slot_tab, weight_tab, slot_hit, weight_hit, codes_pad, codes_ref,
+    slot_tab, weight_tab, slot_hit, weight_hit, codes_ref,
     tok, win, wout, cent, pooled,
     ids_send, ids_got, cent_send, cent_got, row_send, row_got,
     table, acc3, got1, send2, got2, send3, got3,
@@ -198,9 +198,8 @@
     cent_got[me] = cent_send[me]
     cent_recv, cent_sent = exchange(cent_send, cent_got, cent_s, cent_r)
 
-    codes_pad[...] = jnp.full(codes_pad.shape, -1.0, F32)
-    codes_pad[0:passages, 0:codes_in.shape[1]] = codes_in[...].astype(F32)
-    codes_ref[...] = codes_pad[...].T
+    codes_ref[...] = jnp.full(codes_ref.shape, -1.0, F32)
+    codes_ref[0:codes_in.shape[0], 0:passages] = codes_in[...].astype(F32)
 
     pooled[...] = jnp.zeros_like(pooled)
     loads[0].wait()
@@ -410,7 +409,6 @@
             pltpu.VMEM((list_slot.shape[0] // LANES, LANES), F32),
             pltpu.VMEM((padded, LANES), F32),
             pltpu.VMEM((padded, LANES), F32),
-            pltpu.VMEM((padded, LANES), F32),
             pltpu.VMEM((LANES, padded), F32),
             pltpu.VMEM((count * length, width), BF),
             pltpu.VMEM((width, ff), BF),
@@ -438,11 +436,11 @@
             collective_id=0, has_side_effects=True, vmem_limit_bytes=60 * 1024 * 1024),
         name="encode_route",
     )(
-        assign, codes, gain.reshape(1, width),
+        assign, codes.T, gain.reshape(1, width),
         list_slot.reshape(-1, LANES), list_weight.reshape(-1, LANES), tokens.reshape(count * length, width), w_in, w_out, centroids,
     )
 
-    blk = min(512, slots_dev)
+    blk = min(256, slots_dev)
     updated = pl.pallas_call(
         update_kernel,
         grid=(slots_dev // blk,),

time: 60.5 us -> 62.5 us (1.033)
  Pallas kernels: 57.3 us -> 60.7 us
  local copies, waits for them, and re-layouts: 2.1 us -> 0.63 us
    pallas_call x1, Pallas kernels: 10.7 us -> 14.1 us  [shards(): pl.pallas_call(update_kernel, grid=(slots_dev // blk,), out_shape=jax.Sha...]
    unnamed x4 -> x3, local copies, waits for them, and re-layouts: 2.1 us -> 0.63 us
where the time goes in v4:
time: 62.5 us; the launch traced here: 61.9 us
  Pallas kernels  60.7 us (97%)
  between operations  0.65 us (1%)
  local copies, waits for them, and re-layouts  0.63 us (1%)
    pallas_call x1, Pallas kernels, shards(): pl.pallas_call(functools.partial(main_kernel, cfg), out_shape=(jax.ShapeD...  46.5 us
    pallas_call x1, Pallas kernels, shards(): pl.pallas_call(update_kernel, grid=(slots_dev // blk,), out_shape=jax.Sha...  14.1 us

profile of v4, /device:TPU:0, one launch (start us, length us, event | category | flops | bytes accessed | tf_op | source)
XLA Modules:
  0.0 61.9 jit_solution(8359979062278352331)
XLA Ops:
  0.6 46.5 %encode_route.1 = (bf16[256,1024]{1,0:T(8,128)(2,1)}, s32[8,256]{1,0:T(8,128)}, f32[16,1024]{1,0:T(8,128)}) custom-call(s32[96]{0:T(128)} %assign_ref.1, s32[64,96]{1,0:T(8,128)} %bitcast.8, f32[1,1024]{1,0:T(1,128)} %bitcast.9, s32[512,128]{1,0:T(8,128)} %bitcast.6, f32[512,128]{1,0:T(8,128)} %bitcast.7, bf16[768,1024]{1,0:T(8,128)(2,1)} %bitcast.5, ...), custom_call_target="tpu_custom_call" | custom-call | tf_op jit(solution)/shard_map/encode_route/pallas_call | solution.py:398
  47.2 0.0 copy-start
  47.2 14.1 %update_lists.1 = bf16[4096,1024]{1,0:T(8,128)(2,1)} custom-call(s32[8,256]{1,0:T(8,128)} %get-tuple-element.5.ids_ref, bf16[256,1024]{1,0:T(8,128)(2,1)} %get-tuple-element.6.rows_ref, bf16[4096,1024]{1,0:T(8,128)(2,1)} %cent_ref.1), custom_call_target="tpu_custom_call" | custom-call | tf_op jit(solution)/shard_map/update_lists/pallas_call | solution.py:444
  61.3 0.0 copy-done
  61.3 0.6 %copy.12 = f32[16,1024]{1,0:T(8,128)} copy(f32[16,1024]{1,0:T(8,128)S(1)} %copy-done) | data formatting | bytes 131072
Async XLA Ops:
  47.2 14.1 %copy-start = (f32[16,1024]{1,0:T(8,128)S(1)}, f32[16,1024]{1,0:T(8,128)}, u32[]{:S(2)}) copy-start(f32[16,1024]{1,0:T(8,128)} %get-tuple-element.11) | copy-start | bytes 196612
